TPU v7x, 32 devices: a whole 2x2x4 slice. The times are simulated.
32 devices in a mesh: groups: 2 (over y), rows: 4 (over z), heads: 4 (over x, core).
Axes of the slice: x: 2, y: 2, z: 4, core: 2. Of those that a mesh axis runs over, the one named last changes fastest.
Arguments:
- hidden: bfloat16 [2, 2048, 8192], P(None, ('groups', 'rows'), 'heads'), parts along dimension 1, may hold values from -6 to 6
- request_adapter: int32 [2048, 1], P(('groups', 'rows')), parts along dimension 0, may hold values from 0 to 3; in each aligned block of 256 rows (0 to 255, 256 to 511, ...) at most 128 rows name the same one
- adapter_row_index: int32 [4], replicated, may hold values from 0 to 3, each once
- adapter_scales: float32 [4], replicated, may hold values from 0.5 to 2
- down_weight_rows: bfloat16 [4, 128, 8192], P('rows', None, 'heads'), may hold values from -0.0625 to 0.0625
- query_up_weight: bfloat16 [4, 64, 8192], P('rows', None, 'heads'), may hold values from -0.75 to 0.75
- value_up_weight: bfloat16 [4, 64, 1024], P('rows', None, 'heads'), may hold values from -0.75 to 0.75
Outputs:
- delta_q: bfloat16 [2, 2048, 8192], P(None, ('groups', 'rows'), 'heads'), parts along dimension 1
- delta_v: bfloat16 [2, 2048, 1024], P(None, ('groups', 'rows'), 'heads'), parts along dimension 1
There are 2 independent parts, one for each index of `groups`. A program takes and returns all parts, laid end to end along the dimension named above; an argument that names none is the same for every part. Nothing has to cross between parts.
Inputs may be any that keep to these rules, and one draw needn't show every extreme that they name: `request_adapter`: among the 256 requests of one device no adapter is named by more than 128 of them, a bound that some block reaches. `adapter_row_index`: each row of the adapter arrays holds exactly one adapter.
All inputs are finite; a program needn't handle non-finite values.
Results may differ from a plain program's by a relative error of at most 0.005.
Values may be sent and summed in bfloat16 or wider, within the bound.
A program may use at most 64 MiB of HBM per device.

v0:
```python
import jax
import jax.numpy as jnp
from jax import lax
from jax.sharding import PartitionSpec as P


def shrink_rows(received, down_weight):
    flattened = received.reshape(-1, received.shape[-1])
    return lax.dot_general(
        flattened, down_weight, (((1,), (1,)), ((), ())), preferred_element_type=jnp.float32
    )


def expand_rows(summed, scale_value, query_weight, value_weight, shape_lead):
    rank_size = query_weight.shape[0]
    scaled = (summed * scale_value).astype(jnp.bfloat16)
    delta_q = jnp.dot(
        scaled[:, :rank_size], query_weight, preferred_element_type=jnp.float32
    ).astype(jnp.bfloat16)
    delta_v = jnp.dot(
        scaled[:, rank_size:], value_weight, preferred_element_type=jnp.float32
    ).astype(jnp.bfloat16)
    return (
        delta_q.reshape(shape_lead + (query_weight.shape[1],)),
        delta_v.reshape(shape_lead + (value_weight.shape[1],)),
    )


def per_device(
    hidden,
    request_adapter,
    adapter_row_index,
    adapter_scales,
    down_weight_rows,
    query_up_weight,
    value_up_weight,
):
    step_count, rows_here, head_cols = hidden.shape
    holders = lax.axis_size("rows")
    capacity = 2 * rows_here // holders
    adapter_total = adapter_row_index.shape[0]
    down_weight = down_weight_rows[0]
    query_weight = query_up_weight[0]
    value_weight = value_up_weight[0]
    adapter_of = request_adapter[:, 0]
    listing = jnp.arange(adapter_total, dtype=jnp.int32)
    onehot = (adapter_of[:, None] == listing[None, :]).astype(jnp.int32)
    target = jnp.sum(onehot * adapter_row_index[None, :], axis=1)
    own_index = lax.axis_index("rows")
    own_scale = jnp.sum(jnp.where(adapter_row_index == own_index, adapter_scales, 0.0))
    earlier = jnp.cumsum(onehot, axis=0) - onehot
    position = jnp.sum(earlier * onehot, axis=1)
    slot_index = target * capacity + position

    def place_rows(rows_in):
        buffer = jnp.zeros((holders * capacity, head_cols), jnp.bfloat16)
        return buffer.at[slot_index].set(rows_in).reshape(holders, capacity, head_cols)

    def pick_back(returned):
        flattened = returned.reshape(holders * capacity, returned.shape[-1])
        return jnp.take(flattened, slot_index, axis=0)

    outgoing = jnp.stack(
        [place_rows(hidden[step_index]) for step_index in range(step_count)], axis=1
    )
    received = lax.all_to_all(outgoing, "rows", split_axis=0, concat_axis=0, tiled=True)
    summed = lax.psum(shrink_rows(received, down_weight), "heads")
    delta_q, delta_v = expand_rows(
        summed, own_scale, query_weight, value_weight, received.shape[:-1]
    )
    back_q = lax.all_to_all(delta_q, "rows", split_axis=0, concat_axis=0, tiled=True)
    back_v = lax.all_to_all(delta_v, "rows", split_axis=0, concat_axis=0, tiled=True)
    outs_q = [pick_back(back_q[:, step_index]) for step_index in range(step_count)]
    outs_v = [pick_back(back_v[:, step_index]) for step_index in range(step_count)]
    return (jnp.stack(outs_q), jnp.stack(outs_v))


def solution(mesh):
    return jax.shard_map(
        per_device,
        mesh=mesh,
        in_specs=(
            P(None, ("groups", "rows"), "heads"),
            P(("groups", "rows"), None),
            P(),
            P(),
            P("rows", None, "heads"),
            P("rows", None, "heads"),
            P("rows", None, "heads"),
        ),
        out_specs=(P(None, ("groups", "rows"), "heads"), P(None, ("groups", "rows"), "heads")),
        check_vma=False,
    )
```

profile of v0, /device:TPU:0, one launch (start us, length us, event | category | flops | bytes accessed | tf_op | source)
XLA Modules:
  0.0 294.6 jit_solution(4336937956467135135)
XLA Ops:
  7.2 0.0 copy-start
  7.2 0.0 all-reduce.2.cloned.1.call-start
  7.2 0.7 compare_convert_fusion
  8.0 1.2 reduce-window.6
  9.2 0.1 slice.48
  9.2 0.1 copy.11
  9.4 0.1 copy.12
  9.5 0.1 add_bitcast_fusion
  9.6 0.8 select_reduce_fusion
  10.4 3.5 %scatter_custom_fusion.1 = bf16[512,2048]{1,0:T(8,128)(2,1)S(1)} fusion(s32[256]{0:T(256)S(1)} %bitcast.68, bf16[2,256,2048]{2,1,0:T(8,128)(2,1)} %param.11, bf16[]{:T(256)} %constant.23.clone.1), kind=kCustom, calls=%fused_computation.10 | custom fusion | bytes 3146240 | tf_op jit(solution)/shard_map/scatter | solution.py:57
  13.9 4.4 %scatter_custom_fusion = bf16[512,2048]{1,0:T(8,128)(2,1)} fusion(s32[256]{0:T(256)S(1)} %bitcast.69, bf16[2,256,2048]{2,1,0:T(8,128)(2,1)} %param.11, bf16[]{:T(256)} %constant.23.clone.1), kind=kCustom, calls=%fused_computation.12 | custom fusion | bytes 3146240 | tf_op jit(solution)/shard_map/scatter | solution.py:57
  18.3 2.0 pad_maximum_fusion
  20.2 99.3 %all_to_all.15 = bf16[4,2,128,2048]{3,2,1,0:T(8,128)(2,1)S(1)} all-to-all(bf16[4,2,128,2048]{3,2,1,0:T(8,128)(2,1)S(1)} %pad_maximum_fusion), channel_id=1, replica_groups=mesh['groups'=2,'rows'=4,'heads'=4] {'rows'}, dimensions={0} | all-to-all | bytes 8388608 | tf_op jit(solution)/shard_map/all_to_all | solution.py:66
  119.5 0.0 copy-done
  119.5 0.0 copy-start.3
  119.5 0.0 copy-start.4
  119.5 0.0 copy-start.2
  119.5 2.0 fusion.8
  121.6 0.0 copy-start.1
  121.6 0.0 all-reduce.2.cloned.1.call-update
  121.6 0.0 copy-done.3
  121.6 0.0 copy-done.4
  121.6 0.6 fusion.17
  122.2 32.1 %all-reduce.2.cloned.1.call-done = f32[1024,128]{1,0:T(8,128)} async-done(((f32[1024,128]{1,0:T(8,128)}), f32[1024,128]{1,0:T(8,128)}) %all-reduce.2.cloned.1.call-update) | async-done | bytes 524304 | tf_op jit(solution)/shard_map/psum | solution.py:67
  154.3 1.7 multiply_convert_fusion
  156.0 0.0 copy-done.2
  156.0 1.1 convolution_convert_fusion.1
  157.2 4.6 %all-to-all-start.2 = ((bf16[4,2,128,256]{3,2,1,0:T(8,128)(2,1)}), bf16[4,2,128,256]{3,2,1,0:T(8,128)(2,1)S(1)}, u32[]{:S(2)}, u32[]{:S(2)}) async-start(bf16[4,2,128,256]{3,2,1,0:T(8,128)(2,1)} %bitcast.19), calls=%async_computation.2 | async-start | bytes 1048576 | tf_op jit(solution)/shard_map/all_to_all | solution.py:72
  161.8 0.0 copy-done.1
  161.8 3.2 %convolution_convert_fusion = bf16[1024,2048]{1,0:T(8,128)(2,1)} fusion(bf16[1024,128]{1,0:T(8,128)(2,1)S(1)} %multiply_convert_fusion, bf16[1,64,2048]{2,1,0:T(8,128)(2,1)S(1)} %copy-done.1), kind=kOutput, calls=%fused_computation.7 | convolution fusion | flops 270532608 | bytes 4718592 | tf_op jit(solution)/shard_map/dot_general | solution.py:17
  165.0 10.4 %all-to-all-done.2 = bf16[4,2,128,256]{3,2,1,0:T(8,128)(2,1)S(1)} async-done(((bf16[4,2,128,256]{3,2,1,0:T(8,128)(2,1)}), bf16[4,2,128,256]{3,2,1,0:T(8,128)(2,1)S(1)}, u32[]{:S(2)}, u32[]{:S(2)}) %all-to-all-start.2) | async-done | bytes 524320 | tf_op jit(solution)/shard_map/all_to_all | solution.py:72
  175.3 5.0 %all-to-all-start.1 = ((bf16[4,2,128,2048]{3,2,1,0:T(8,128)(2,1)}), bf16[4,2,128,2048]{3,2,1,0:T(8,128)(2,1)}, u32[]{:S(2)}, u32[]{:S(2)}) async-start(bf16[4,2,128,2048]{3,2,1,0:T(8,128)(2,1)} %bitcast.58), calls=%async_computation.1 | async-start | bytes 8388608 | tf_op jit(solution)/shard_map/all_to_all | solution.py:71
  180.4 1.2 gather_fusion.2
  181.6 1.2 gather_fusion.3
  182.8 0.1 select_bitcast_fusion.3
  182.9 0.7 pad_maximum_fusion.2
  183.6 89.3 %all-to-all-done.1 = bf16[4,2,128,2048]{3,2,1,0:T(8,128)(2,1)} async-done(((bf16[4,2,128,2048]{3,2,1,0:T(8,128)(2,1)}), bf16[4,2,128,2048]{3,2,1,0:T(8,128)(2,1)}, u32[]{:S(2)}, u32[]{:S(2)}) %all-to-all-start.1) | async-done | bytes 4194336 | tf_op jit(solution)/shard_map/all_to_all | solution.py:71
  272.9 4.0 %fusion.18 = (bf16[4,1,128,2048]{3,2,1,0:T(8,128)(2,1)}, bf16[4,1,128,2048]{3,2,1,0:T(8,128)(2,1)S(1)}) fusion(bf16[4,2,128,2048]{3,2,1,0:T(8,128)(2,1)} %all-to-all-done.1), kind=kLoop, calls=%fused_computation.45 | loop fusion | bytes 8388608 | tf_op jit(solution)/shard_map/slice | solution.py:73
  276.9 5.2 %gather_fusion = bf16[256,2048]{1,0:T(8,128)(2,1)} fusion(bf16[512,2048]{1,0:T(8,128)(2,1)} %bitcast.57, s32[1024]{0:T(1024)S(1)} %pad_clamp_fusion), kind=kCustom, calls=%fused_computation.clone | custom fusion | bytes 2098176 | tf_op jit(solution)/shard_map/jit(_take)/gather | solution.py:61
  282.1 2.3 gather_fusion.1
  284.4 1.8 select_bitcast_fusion.1
  286.2 1.5 pad_maximum_fusion.1
  (7 shorter events, 0.1 us)
Async XLA Ops:
  7.2 112.3 %copy-start = (bf16[1,128,2048]{2,1,0:T(8,128)(2,1)S(1)}, bf16[1,128,2048]{2,1,0:T(8,128)(2,1)}, u32[]{:S(2)}) copy-start(bf16[1,128,2048]{2,1,0:T(8,128)(2,1)} %param.15) | copy-start | bytes 1572868
  7.2 147.1 %all-reduce.2.cloned.1.call-start = ((), (), s32[]{:S(2)}) async-start(), calls=%async_computation.3 | async-start | bytes 1048576 | tf_op jit(solution)/shard_map/psum | solution.py:67
  119.5 2.1 copy-start.3
  119.5 2.1 copy-start.4
  119.5 36.5 %copy-start.2 = (bf16[1,64,256]{2,1,0:T(8,128)(2,1)S(1)}, bf16[1,64,256]{2,1,0:T(8,128)(2,1)}, u32[]{:S(2)}) copy-start(bf16[1,64,256]{2,1,0:T(8,128)(2,1)} %param.17) | copy-start | bytes 98308
  121.6 40.2 %copy-start.1 = (bf16[1,64,2048]{2,1,0:T(8,128)(2,1)S(1)}, bf16[1,64,2048]{2,1,0:T(8,128)(2,1)}, u32[]{:S(2)}) copy-start(bf16[1,64,2048]{2,1,0:T(8,128)(2,1)} %param.16) | copy-start | bytes 786436
  157.2 18.2 %all-to-all-start.2 = ((bf16[4,2,128,256]{3,2,1,0:T(8,128)(2,1)}), bf16[4,2,128,256]{3,2,1,0:T(8,128)(2,1)S(1)}, u32[]{:S(2)}, u32[]{:S(2)}) async-start(bf16[4,2,128,256]{3,2,1,0:T(8,128)(2,1)} %bitcast.19), calls=%async_computation.2 | async-start | bytes 1048576 | tf_op jit(solution)/shard_map/all_to_all | solution.py:72
  175.3 97.6 %all-to-all-start.1 = ((bf16[4,2,128,2048]{3,2,1,0:T(8,128)(2,1)}), bf16[4,2,128,2048]{3,2,1,0:T(8,128)(2,1)}, u32[]{:S(2)}, u32[]{:S(2)}) async-start(bf16[4,2,128,2048]{3,2,1,0:T(8,128)(2,1)} %bitcast.58), calls=%async_computation.1 | async-start | bytes 8388608 | tf_op jit(solution)/shard_map/all_to_all | solution.py:71
Sparse Core Ops, SparseCore 0:
  121.7 32.5 all-reduce.1
where the time goes:
time: 295 us
  waiting for transfers between devices  132 us (45%)
  blocking collectives  99.3 us (34%)
  local copies, waits for them, and re-layouts  22.1 us (7%)
  between operations  14.1 us (5%)
  other arithmetic  11.3 us (4%)
  starting transfers between devices  9.67 us (3%)
  matrix products  6.4 us (2%)
    all_to_all x1, blocking collectives, per_device(): lax.all_to_all(outgoing, 'rows', split_axis=0, concat_axis=0, tiled=True)  99.3 us
    all_to_all x1, waiting for transfers between devices, per_device(): lax.all_to_all(delta_q, 'rows', split_axis=0, concat_axis=0, tiled=True)  89.3 us
    psum x1, waiting for transfers between devices, per_device(): summed = lax.psum(shrink_rows(received, down_weight), 'heads')  32.1 us
    all_to_all x1, waiting for transfers between devices, per_device(): lax.all_to_all(delta_v, 'rows', split_axis=0, concat_axis=0, tiled=True)  10.4 us
    gather x4, local copies, waits for them, and re-layouts, pick_back(): return jnp.take(flattened, slot_index, axis=0)  9.84 us
    scatter x2, local copies, waits for them, and re-layouts, place_rows(): buffer.at[slot_index].set(rows_in).reshape(holders, capacity, head_cols)  7.9 us
  transfers between devices with their start and end apart: 3, of which 3 were waited for; matrix products, arithmetic and copies ran while one was open for 2% of the time, Pallas kernels for 0%

commit v1 on v0

--- a/solution.py
+++ b/solution.py
@@ -1,7 +1,368 @@
+import functools
+
 import jax
 import jax.numpy as jnp
 from jax import lax
+from jax.experimental import pallas as pl
+from jax.experimental.pallas import tpu as pltpu
 from jax.sharding import PartitionSpec as P
+
+DOWN_CHUNKS = 2
+UP_CHUNKS = 2
+MESH = pl.DeviceIdType.MESH
+
+
+def lora_kernel(
+    holders,
+    row_index_ref,
+    scales_ref,
+    adapter_ref,
+    hidden_hbm,
+    down_hbm,
+    query_hbm,
+    value_hbm,
+    out_q_hbm,
+    out_v_hbm,
+    hidden_ref,
+    down_all,
+    query_all,
+    value_all,
+    acc_ref,
+    core_buf,
+    pair_sum,
+    chip_buf,
+    scaled_ref,
+    target_ref,
+    scale_ref,
+    stage_q,
+    stage_v,
+    local_sem,
+    z_send,
+    z_recv,
+    y_send,
+    y_recv,
+    h_send,
+    h_recv,
+    out_sem,
+):
+    steps, rows_here, cols = hidden_hbm.shape
+    rank2 = down_hbm.shape[1]
+    rank = query_hbm.shape[1]
+    width_q = query_hbm.shape[2]
+    group = lax.axis_index("groups")
+    me = lax.axis_index("rows")
+    head = lax.axis_index("heads")
+    core = head % 2
+    sibling = head + 1 - 2 * core
+    across = (head + 2) % 4
+    other_group = 1 - group
+    half_d = rank2 // 2
+    half_u = rank // 2
+    chunk_d = half_d // DOWN_CHUNKS
+    chunk_u = width_q // UP_CHUNKS
+    pieces_d = [("d", c) for c in range(DOWN_CHUNKS)]
+    pieces_u = [("v", 0)] + [("q", c) for c in range(UP_CHUNKS)]
+    slot_of = {piece: at for at, piece in enumerate(pieces_d + pieces_u)}
+    far = range(1, holders)
+
+    def origin_of(way, dist):
+        return me - dist if way == 0 else me + dist
+
+    def exists(origin):
+        return jnp.logical_and(origin >= 0, origin < holders)
+
+    def view(ref, lead, piece, half):
+        kind, c = piece
+        if kind == "d":
+            start = pl.multiple_of(half * half_d + c * chunk_d, 16)
+            return ref.at[lead, pl.ds(start, chunk_d), :]
+        start = pl.multiple_of(half * half_u, 16)
+        if kind == "v":
+            return ref.at[lead, pl.ds(start, half_u), :]
+        return ref.at[lead, pl.ds(start, half_u), pl.ds(c * chunk_u, chunk_u)]
+
+    own_of = {"d": down_hbm, "q": query_hbm, "v": value_hbm}
+    all_of = {"d": down_all, "q": query_all, "v": value_all}
+
+    def z_copy(way, dist, piece):
+        origin = me - (dist - 1) if way == 0 else me + (dist - 1)
+        to = me + 1 if way == 0 else me - 1
+        dst = view(all_of[piece[0]], origin, piece, group)
+        src = view(own_of[piece[0]], 0, piece, group) if dist == 1 else dst
+        return pltpu.make_async_remote_copy(
+            src_ref=src,
+            dst_ref=dst,
+            send_sem=z_send.at[way, dist - 1, slot_of[piece]],
+            recv_sem=z_recv.at[way, dist - 1, slot_of[piece]],
+            device_id={"rows": to},
+            device_id_type=MESH,
+        )
+
+    def z_arrival(way, dist, piece):
+        dst = view(all_of[piece[0]], origin_of(way, dist), piece, group)
+        return pltpu.make_async_remote_copy(
+            src_ref=dst,
+            dst_ref=dst,
+            send_sem=z_send.at[way, dist - 1, slot_of[piece]],
+            recv_sem=z_recv.at[way, dist - 1, slot_of[piece]],
+            device_id={"rows": me + 1 if way == 0 else me - 1},
+            device_id_type=MESH,
+        )
+
+    def y_copy(way, dist, piece, half):
+        ref = view(all_of[piece[0]], origin_of(way, dist), piece, half)
+        return pltpu.make_async_remote_copy(
+            src_ref=ref,
+            dst_ref=ref,
+            send_sem=y_send.at[way, dist - 1, slot_of[piece]],
+            recv_sem=y_recv.at[way, dist - 1, slot_of[piece]],
+            device_id={"groups": other_group},
+            device_id_type=MESH,
+        )
+
+    def h_copy(stage, src, dst, to):
+        return pltpu.make_async_remote_copy(
+            src_ref=src,
+            dst_ref=dst,
+            send_sem=h_send.at[stage],
+            recv_sem=h_recv.at[stage],
+            device_id={"heads": to},
+            device_id_type=MESH,
+        )
+
+    def next_exists(way):
+        return me < holders - 1 if way == 0 else me > 0
+
+    def start_own(pieces):
+        for way in (0, 1):
+            @pl.when(next_exists(way))
+            def _():
+                for piece in pieces:
+                    z_copy(way, 1, piece).start()
+
+    def take_z(dist, pieces):
+        for piece in pieces:
+            for way in (0, 1):
+                @pl.when(exists(origin_of(way, dist)))
+                def _():
+                    z_arrival(way, dist, piece).wait_recv()
+                    if dist < holders - 1:
+                        @pl.when(next_exists(way))
+                        def _():
+                            z_copy(way, dist + 1, piece).start()
+                    y_copy(way, dist, piece, group).start()
+
+    def take_y(dist, pieces):
+        for way in (0, 1):
+            @pl.when(exists(origin_of(way, dist)))
+            def _():
+                for piece in pieces:
+                    y_copy(way, dist, piece, other_group).wait_recv()
+
+    local = [
+        pltpu.make_async_copy(hidden_hbm, hidden_ref, local_sem.at[0]),
+        pltpu.make_async_copy(down_hbm.at[0], down_all.at[me], local_sem.at[1]),
+        pltpu.make_async_copy(query_hbm.at[0], query_all.at[me], local_sem.at[2]),
+        pltpu.make_async_copy(value_hbm.at[0], value_all.at[me], local_sem.at[3]),
+    ]
+    for copy in local:
+        copy.start()
+
+    barrier = pltpu.get_barrier_semaphore()
+    for way in (0, 1):
+        @pl.when(next_exists(way))
+        def _():
+            pl.semaphore_signal(
+                barrier, inc=1, device_id={"rows": me + 1 - 2 * way}, device_id_type=MESH
+            )
+    pl.semaphore_signal(barrier, inc=1, device_id={"groups": other_group}, device_id_type=MESH)
+    for to in (sibling, across):
+        pl.semaphore_signal(barrier, inc=1, device_id={"heads": to}, device_id_type=MESH)
+    neighbours = (me > 0).astype(jnp.int32) + (me < holders - 1).astype(jnp.int32)
+    pl.semaphore_wait(barrier, neighbours + 3)
+
+    start_own(pieces_d)
+
+    adapters = adapter_ref[...]
+    target = jnp.zeros_like(adapters)
+    scale = jnp.zeros(adapters.shape, jnp.float32)
+    for a in range(row_index_ref.shape[0]):
+        target = jnp.where(adapters == a, row_index_ref[a], target)
+        scale = jnp.where(adapters == a, scales_ref[a], scale)
+    target_ref[...] = jnp.broadcast_to(target, target_ref.shape)
+    scale_ref[...] = jnp.broadcast_to(scale, scale_ref.shape)
+
+    def shrink(origin, first=False):
+        weight = down_all[origin]
+        for step in range(steps):
+            part = lax.dot_general(
+                hidden_ref[step],
+                weight,
+                (((1,), (1,)), ((), ())),
+                preferred_element_type=jnp.float32,
+            )
+            kept = 0.0 if first else acc_ref[step]
+            acc_ref[step] = jnp.where(target_ref[...] == origin, part, kept)
+
+    def shrink_far(dist):
+        for way in (0, 1):
+            @pl.when(exists(origin_of(way, dist)))
+            def _():
+                shrink(origin_of(way, dist))
+
+    local[0].wait()
+    local[1].wait()
+    shrink(me, first=True)
+    for dist in far:
+        take_z(dist, pieces_d)
+        if dist == max(1, holders - 2):
+            start_own(pieces_u)
+        if dist > 1:
+            take_y(dist - 1, pieces_d)
+            shrink_far(dist - 1)
+    take_y(holders - 1, pieces_d)
+    shrink_far(holders - 1)
+
+    to_core = h_copy(0, acc_ref.at[1 - core], core_buf, sibling)
+    to_chip = h_copy(1, pair_sum, chip_buf, across)
+    to_core_back = h_copy(2, scaled_ref.at[core], scaled_ref.at[core], sibling)
+    from_core_back = h_copy(2, scaled_ref.at[1 - core], scaled_ref.at[1 - core], sibling)
+
+    to_core.start()
+    take_z(1, pieces_u)
+    to_core.wait_recv()
+    pair_sum[...] = acc_ref[core] + core_buf[...]
+    to_chip.start()
+    for dist in range(2, holders - 1):
+        take_z(dist, pieces_u)
+    to_chip.wait_recv()
+    scaled_ref[core] = ((pair_sum[...] + chip_buf[...]) * scale_ref[...]).astype(jnp.bfloat16)
+    to_core_back.start()
+    take_z(holders - 1, pieces_u)
+    from_core_back.wait_recv()
+
+    lane = lax.broadcasted_iota(jnp.int32, target_ref.shape, 1)
+    low = lane < rank
+    lefts = []
+    for step in range(steps):
+        both = scaled_ref[step].astype(jnp.float32)
+        swapped = pltpu.roll(both, rank, 1)
+        pair = []
+        for doubled in (jnp.where(low, both, swapped), jnp.where(low, swapped, both)):
+            blocks = []
+            for k in range(holders // 2):
+                mine = target_ref[...] == jnp.where(low, 2 * k, 2 * k + 1)
+                blocks.append(jnp.where(mine, doubled, 0.0).astype(jnp.bfloat16))
+            pair.append(jnp.concatenate(blocks, axis=1))
+        lefts.append(pair)
+
+    local[2].wait()
+    local[3].wait()
+    outs = []
+    for piece in pieces_u:
+        for dist in far:
+            take_y(dist, [piece])
+        at = pl.ds(0, value_all.shape[2]) if piece[0] == "v" else pl.ds(piece[1] * chunk_u, chunk_u)
+        source, stage, out = (
+            (value_all, stage_v, out_v_hbm) if piece[0] == "v" else (query_all, stage_q, out_q_hbm)
+        )
+        which = 1 if piece[0] == "v" else 0
+        right = source[:, :, at]
+        right = right.reshape(holders * rank, right.shape[2])
+        for step in range(steps):
+            stage[step, :, at] = jnp.dot(
+                lefts[step][which], right, preferred_element_type=jnp.float32
+            ).astype(jnp.bfloat16)
+            copy = pltpu.make_async_copy(
+                stage.at[step, :, at], out.at[step, :, at], out_sem.at[len(outs)]
+            )
+            copy.start()
+            outs.append(copy)
+
+    for pieces in (pieces_d, pieces_u):
+        for dist in far:
+            for way in (0, 1):
+                origin = me - (dist - 1) if way == 0 else me + (dist - 1)
+
+                @pl.when(jnp.logical_and(exists(origin), next_exists(way)))
+                def _():
+                    for piece in pieces:
+                        z_copy(way, dist, piece).wait_send()
+
+                @pl.when(exists(origin_of(way, dist)))
+                def _():
+                    for piece in pieces:
+                        y_copy(way, dist, piece, group).wait_send()
+    to_core.wait_send()
+    to_chip.wait_send()
+    to_core_back.wait_send()
+    for copy in outs:
+        copy.wait()
+
+
+def per_device_weights(
+    hidden,
+    request_adapter,
+    adapter_row_index,
+    adapter_scales,
+    down_weight_rows,
+    query_up_weight,
+    value_up_weight,
+):
+    steps, rows_here, cols = hidden.shape
+    holders = lax.axis_size("rows")
+    rank2 = down_weight_rows.shape[1]
+    rank = query_up_weight.shape[1]
+    width_q, width_v = query_up_weight.shape[2], value_up_weight.shape[2]
+    slots = DOWN_CHUNKS + UP_CHUNKS + 1
+    bf16, f32 = jnp.bfloat16, jnp.float32
+    smem = pl.BlockSpec(memory_space=pltpu.SMEM)
+    vmem = pl.BlockSpec(memory_space=pltpu.VMEM)
+    anyw = pl.BlockSpec(memory_space=pl.ANY)
+    return pl.pallas_call(
+        functools.partial(lora_kernel, holders),
+        out_shape=(
+            jax.ShapeDtypeStruct((steps, rows_here, width_q), bf16),
+            jax.ShapeDtypeStruct((steps, rows_here, width_v), bf16),
+        ),
+        in_specs=[smem, smem, vmem, anyw, anyw, anyw, anyw],
+        out_specs=(anyw, anyw),
+        scratch_shapes=[
+            pltpu.VMEM((steps, rows_here, cols), bf16),
+            pltpu.VMEM((holders, rank2, cols), bf16),
+            pltpu.VMEM((holders, rank, width_q), bf16),
+            pltpu.VMEM((holders, rank, width_v), bf16),
+            pltpu.VMEM((steps, rows_here, rank2), f32),
+            pltpu.VMEM((rows_here, rank2), f32),
+            pltpu.VMEM((rows_here, rank2), f32),
+            pltpu.VMEM((rows_here, rank2), f32),
+            pltpu.VMEM((steps, rows_here, rank2), bf16),
+            pltpu.VMEM((rows_here, rank2), jnp.int32),
+            pltpu.VMEM((rows_here, rank2), f32),
+            pltpu.VMEM((steps, rows_here, width_q), bf16),
+            pltpu.VMEM((steps, rows_here, width_v), bf16),
+            pltpu.SemaphoreType.DMA((4,)),
+            pltpu.SemaphoreType.DMA((2, holders - 1, slots)),
+            pltpu.SemaphoreType.DMA((2, holders - 1, slots)),
+            pltpu.SemaphoreType.DMA((2, holders - 1, slots)),
+            pltpu.SemaphoreType.DMA((2, holders - 1, slots)),
+            pltpu.SemaphoreType.DMA((3,)),
+            pltpu.SemaphoreType.DMA((3,)),
+            pltpu.SemaphoreType.DMA((steps * (UP_CHUNKS + 1),)),
+        ],
+        compiler_params=pltpu.CompilerParams(
+            collective_id=0, has_side_effects=True, vmem_limit_bytes=32 * 1024 * 1024
+        ),
+        name="lora_weights",
+    )(
+        adapter_row_index,
+        adapter_scales,
+        request_adapter,
+        hidden,
+        down_weight_rows,
+        query_up_weight,
+        value_up_weight,
+    )
 
 
 def shrink_rows(received, down_weight):
@@ -26,7 +387,7 @@
     )
 
 
-def per_device(
+def per_device_rows(
     hidden,
     request_adapter,
     adapter_row_index,
@@ -75,6 +436,40 @@
     return (jnp.stack(outs_q), jnp.stack(outs_v))
 
 
+def per_device(
+    hidden,
+    request_adapter,
+    adapter_row_index,
+    adapter_scales,
+    down_weight_rows,
+    query_up_weight,
+    value_up_weight,
+):
+    steps, rows_here, cols = hidden.shape
+    holders = lax.axis_size("rows")
+    rank2 = down_weight_rows.shape[1]
+    width = query_up_weight.shape[2] + value_up_weight.shape[2]
+    by_weights = holders * (rank2 * cols + rank2 // 2 * width)
+    by_rows = 2 * steps * rows_here * (cols + width)
+    fits = (
+        lax.axis_size("groups") == 2
+        and lax.axis_size("heads") == 4
+        and holders % 2 == 0
+        and steps == 2
+        and rank2 == 128
+    )
+    plan = per_device_weights if fits and by_weights < by_rows else per_device_rows
+    return plan(
+        hidden,
+        request_adapter,
+        adapter_row_index,
+        adapter_scales,
+        down_weight_rows,
+        query_up_weight,
+        value_up_weight,
+    )
+
+
 def solution(mesh):
     return jax.shard_map(
         per_device,

time: 295 us -> 51.5 us (0.17)
  waiting for transfers between devices: 132 us -> 0 us
  blocking collectives: 99.3 us -> 0 us
  Pallas kernels: 0 us -> 42 us
  local copies, waits for them, and re-layouts: 22.1 us -> 8.48 us
  between operations: 14.1 us -> 0.66 us
  other arithmetic: 11.3 us -> 0 us
  starting transfers between devices: 9.67 us -> 0 us
  matrix products: 6.4 us -> 0 us
    all_to_all x2 -> x0, waiting for transfers between devices: 99.7 us -> none  [the longest x1 89.3 us: per_device(): lax.all_to_all(delta_q, 'rows', split_axis=0, concat_axis=0, tiled=True)]
    all_to_all x1 -> x0, blocking collectives: 99.3 us -> none  [per_device(): lax.all_to_all(outgoing, 'rows', split_axis=0, concat_axis=0, tiled=True)]
    pallas_call x0 -> x1, Pallas kernels: none -> 42 us  [per_device_weights(): pl.pallas_call(functools.partial(lora_kernel, holders), out_shape=(jax.Sh...]
    psum x1 -> x0, waiting for transfers between devices: 32.1 us -> none  [per_device(): summed = lax.psum(shrink_rows(received, down_weight), 'heads')]
    gather x4 -> x0, local copies, waits for them, and re-layouts: 9.84 us -> none  [pick_back(): return jnp.take(flattened, slot_index, axis=0)]
    all_to_all x2 -> x0, starting transfers between devices: 9.64 us -> none  [the longest x1 5.04 us: per_device(): lax.all_to_all(delta_q, 'rows', split_axis=0, concat_axis=0, tiled=True)]
    unnamed x10 -> x15, local copies, waits for them, and re-layouts: 0.02 us -> 8.48 us
    scatter x2 -> x0, local copies, waits for them, and re-layouts: 7.9 us -> none  [place_rows(): buffer.at[slot_index].set(rows_in).reshape(holders, capacity, head_cols)]
  transfers between devices with their start and end apart: 3 -> 0, of which waited for: 3 -> 0; matrix products, arithmetic and copies ran while one was open for 2% -> 0% of each run, Pallas kernels for 0% -> 0%
where the time goes in v1:
time: 51.5 us; the launch traced here: 51.1 us
  Pallas kernels  42 us (82%)
  local copies, waits for them, and re-layouts  8.48 us (16%)
  between operations  0.66 us (1%)
    pallas_call x1, Pallas kernels, per_device_weights(): pl.pallas_call(functools.partial(lora_kernel, holders), out_shape=(jax.Sh...  42 us
    unnamed x15, local copies, waits for them, and re-layouts  8.48 us

profile of v1, /device:TPU:0, one launch (start us, length us, event | category | flops | bytes accessed | tf_op | source)
XLA Modules:
  0.0 51.1 jit_solution(17840207528365965714)
XLA Ops:
  0.6 0.8 %copy.9.adapter_ref = s32[256,1]{1,0:T(8,128)S(1)} copy(s32[256,1]{0,1:T(1,128)} %param.8) | data formatting | bytes 2048 | tf_op args[1]
  1.4 0.0 copy-start
  1.5 1.6 %copy-done = bf16[2,256,2048]{2,1,0:T(8,128)(2,1)S(1)} copy-done((bf16[2,256,2048]{2,1,0:T(8,128)(2,1)S(1)}, bf16[2,256,2048]{2,1,0:T(8,128)(2,1)}, u32[]{:S(2)}) %copy-start) | copy-done | bytes 2097176
  3.0 0.0 copy-start.1
  3.0 1.0 %copy-done.1 = bf16[1,128,2048]{2,1,0:T(8,128)(2,1)S(1)} copy-done((bf16[1,128,2048]{2,1,0:T(8,128)(2,1)S(1)}, bf16[1,128,2048]{2,1,0:T(8,128)(2,1)}, u32[]{:S(2)}) %copy-start.1) | copy-done | bytes 524312
  4.1 0.0 copy-start.2
  4.1 0.9 %copy-done.2 = bf16[1,64,2048]{2,1,0:T(8,128)(2,1)S(1)} copy-done((bf16[1,64,2048]{2,1,0:T(8,128)(2,1)S(1)}, bf16[1,64,2048]{2,1,0:T(8,128)(2,1)}, u32[]{:S(2)}) %copy-start.2) | copy-done | bytes 262168
  5.0 0.0 copy-start.3
  5.0 0.8 %copy-done.3 = bf16[1,64,256]{2,1,0:T(8,128)(2,1)S(1)} copy-done((bf16[1,64,256]{2,1,0:T(8,128)(2,1)S(1)}, bf16[1,64,256]{2,1,0:T(8,128)(2,1)}, u32[]{:S(2)}) %copy-start.3) | copy-done | bytes 32792
  5.8 0.0 copy-start.4
  5.8 0.7 %copy-done.4 = s32[4]{0:T(128)S(1)} copy-done((s32[4]{0:T(128)S(1)}, s32[4]{0:T(128)}, u32[]{:S(2)}) %copy-start.4) | copy-done | bytes 40
  6.4 0.0 copy-start.5
  6.4 0.7 %copy-done.5 = f32[4]{0:T(128)S(1)} copy-done((f32[4]{0:T(128)S(1)}, f32[4]{0:T(128)}, u32[]{:S(2)}) %copy-start.5) | copy-done | bytes 40
  7.1 42.0 %lora_weights.1 = (bf16[2,256,2048]{2,1,0:T(8,128)(2,1)S(1)}, bf16[2,256,256]{2,1,0:T(8,128)(2,1)S(1)}) custom-call(s32[4]{0:T(128)S(1)} %copy-done.4, f32[4]{0:T(128)S(1)} %copy-done.5, s32[256,1]{1,0:T(8,128)S(1)} %copy.9.adapter_ref, bf16[2,256,2048]{2,1,0:T(8,128)(2,1)S(1)} %copy-done, bf16[1,128,2048]{2,1,0:T(8,128)(2,1)S(1)} %copy-done.1, ...), custom_call_target="tpu_custom_call" | custom-call | tf_op jit(solution)/shard_map/lora_weights/pallas_call | solution.py:322
  49.1 1.3 %copy.12 = bf16[2,256,2048]{2,1,0:T(8,128)(2,1)} copy(bf16[2,256,2048]{2,1,0:T(8,128)(2,1)S(1)} %get-tuple-element.4) | data formatting | bytes 4194304
  50.4 0.7 %copy.13 = bf16[2,256,256]{2,1,0:T(8,128)(2,1)} copy(bf16[2,256,256]{2,1,0:T(8,128)(2,1)S(1)} %get-tuple-element.5) | data formatting | bytes 524288
Async XLA Ops:
  1.4 1.6 %copy-start = (bf16[2,256,2048]{2,1,0:T(8,128)(2,1)S(1)}, bf16[2,256,2048]{2,1,0:T(8,128)(2,1)}, u32[]{:S(2)}) copy-start(bf16[2,256,2048]{2,1,0:T(8,128)(2,1)} %hidden_hbm.1) | copy-start | bytes 6291460
  3.0 1.0 %copy-start.1 = (bf16[1,128,2048]{2,1,0:T(8,128)(2,1)S(1)}, bf16[1,128,2048]{2,1,0:T(8,128)(2,1)}, u32[]{:S(2)}) copy-start(bf16[1,128,2048]{2,1,0:T(8,128)(2,1)} %down_hbm.1) | copy-start | bytes 1572868
  4.1 0.9 %copy-start.2 = (bf16[1,64,2048]{2,1,0:T(8,128)(2,1)S(1)}, bf16[1,64,2048]{2,1,0:T(8,128)(2,1)}, u32[]{:S(2)}) copy-start(bf16[1,64,2048]{2,1,0:T(8,128)(2,1)} %query_hbm.1) | copy-start | bytes 786436
  5.0 0.8 %copy-start.3 = (bf16[1,64,256]{2,1,0:T(8,128)(2,1)S(1)}, bf16[1,64,256]{2,1,0:T(8,128)(2,1)}, u32[]{:S(2)}) copy-start(bf16[1,64,256]{2,1,0:T(8,128)(2,1)} %value_hbm.1) | copy-start | bytes 98308
  5.8 0.7 %copy-start.4 = (s32[4]{0:T(128)S(1)}, s32[4]{0:T(128)}, u32[]{:S(2)}) copy-start(s32[4]{0:T(128)} %row_index_ref.1) | copy-start | bytes 52
  6.4 0.7 %copy-start.5 = (f32[4]{0:T(128)S(1)}, f32[4]{0:T(128)}, u32[]{:S(2)}) copy-start(f32[4]{0:T(128)} %scales_ref.1) | copy-start | bytes 52

commit v2 on v1

--- a/solution.py
+++ b/solution.py
@@ -7,8 +7,8 @@
 from jax.experimental.pallas import tpu as pltpu
 from jax.sharding import PartitionSpec as P
 
-DOWN_CHUNKS = 2
-UP_CHUNKS = 2
+DOWN_CHUNKS = 4
+UP_CHUNKS = 4
 MESH = pl.DeviceIdType.MESH
 
 
@@ -30,6 +30,7 @@
     acc_ref,
     core_buf,
     pair_sum,
+    pair_out,
     chip_buf,
     scaled_ref,
     target_ref,
@@ -224,7 +225,7 @@
     shrink_far(holders - 1)
 
     to_core = h_copy(0, acc_ref.at[1 - core], core_buf, sibling)
-    to_chip = h_copy(1, pair_sum, chip_buf, across)
+    to_chip = h_copy(1, pair_out, chip_buf, across)
     to_core_back = h_copy(2, scaled_ref.at[core], scaled_ref.at[core], sibling)
     from_core_back = h_copy(2, scaled_ref.at[1 - core], scaled_ref.at[1 - core], sibling)
 
@@ -232,11 +233,12 @@
     take_z(1, pieces_u)
     to_core.wait_recv()
     pair_sum[...] = acc_ref[core] + core_buf[...]
+    pair_out[...] = pair_sum[...].astype(jnp.bfloat16)
     to_chip.start()
     for dist in range(2, holders - 1):
         take_z(dist, pieces_u)
     to_chip.wait_recv()
-    scaled_ref[core] = ((pair_sum[...] + chip_buf[...]) * scale_ref[...]).astype(jnp.bfloat16)
+    scaled_ref[core] = ((pair_sum[...] + chip_buf[...].astype(jnp.float32)) * scale_ref[...]).astype(jnp.bfloat16)
     to_core_back.start()
     take_z(holders - 1, pieces_u)
     from_core_back.wait_recv()
@@ -335,7 +337,8 @@
             pltpu.VMEM((steps, rows_here, rank2), f32),
             pltpu.VMEM((rows_here, rank2), f32),
             pltpu.VMEM((rows_here, rank2), f32),
-            pltpu.VMEM((rows_here, rank2), f32),
+            pltpu.VMEM((rows_here, rank2), bf16),
+            pltpu.VMEM((rows_here, rank2), bf16),
             pltpu.VMEM((steps, rows_here, rank2), bf16),
             pltpu.VMEM((rows_here, rank2), jnp.int32),
             pltpu.VMEM((rows_here, rank2), f32),
@@ -351,7 +354,7 @@
             pltpu.SemaphoreType.DMA((steps * (UP_CHUNKS + 1),)),
         ],
         compiler_params=pltpu.CompilerParams(
-            collective_id=0, has_side_effects=True, vmem_limit_bytes=32 * 1024 * 1024
+            collective_id=0, has_side_effects=True, vmem_limit_bytes=60 * 1024 * 1024
         ),
         name="lora_weights",
     )(

time: 51.5 us -> 48.1 us (0.934)
  local copies, waits for them, and re-layouts: 8.48 us -> 5.38 us
    unnamed x15 -> x5, local copies, waits for them, and re-layouts: 8.48 us -> 5.38 us
where the time goes in v2:
time: 48.1 us; the launch traced here: 47.9 us
  Pallas kernels  41.8 us (87%)
  local copies, waits for them, and re-layouts  5.38 us (11%)
  between operations  0.65 us (1%)
    pallas_call x1, Pallas kernels, per_device_weights(): pl.pallas_call(functools.partial(lora_kernel, holders), out_shape=(jax.Sh...  41.8 us
    unnamed x5, local copies, waits for them, and re-layouts  5.38 us

profile of v2, /device:TPU:0, one launch (start us, length us, event | category | flops | bytes accessed | tf_op | source)
XLA Modules:
  0.0 47.9 jit_solution(8061701552870508089)
XLA Ops:
  0.6 1.5 %copy.9.adapter_ref = s32[256,1]{1,0:T(8,128)} copy(s32[256,1]{0,1:T(1,128)} %param.8) | data formatting | bytes 2048 | tf_op args[1]
  2.1 41.8 %lora_weights.1 = (bf16[2,256,2048]{2,1,0:T(8,128)(2,1)}, bf16[2,256,256]{2,1,0:T(8,128)(2,1)}) custom-call(s32[4]{0:T(128)} %row_index_ref.1, f32[4]{0:T(128)} %scales_ref.1, s32[256,1]{1,0:T(8,128)} %copy.9.adapter_ref, bf16[2,256,2048]{2,1,0:T(8,128)(2,1)} %hidden_hbm.1, bf16[1,128,2048]{2,1,0:T(8,128)(2,1)} %down_hbm.1, bf16[1,64,2048]{2,1,0:T(8,128)(2,1)} %query_hbm.1, ...), custom_call_target="tpu_custom_call" | custom-call | tf_op jit(solution)/shard_map/lora_weights/pallas_call | solution.py:324
  44.0 0.0 copy-start
  44.0 3.2 %copy.12 = bf16[2,256,2048]{2,1,0:T(8,128)(2,1)} copy(bf16[2,256,2048]{2,1,0:T(8,128)(2,1)} %get-tuple-element.4) | data formatting | bytes 4194304
  47.2 0.0 copy-done
  47.2 0.7 %copy.13 = bf16[2,256,256]{2,1,0:T(8,128)(2,1)} copy(bf16[2,256,256]{2,1,0:T(8,128)(2,1)S(1)} %copy-done) | data formatting | bytes 524288
Async XLA Ops:
  44.0 3.2 %copy-start = (bf16[2,256,256]{2,1,0:T(8,128)(2,1)S(1)}, bf16[2,256,256]{2,1,0:T(8,128)(2,1)}, u32[]{:S(2)}) copy-start(bf16[2,256,256]{2,1,0:T(8,128)(2,1)} %get-tuple-element.5) | copy-start | bytes 786436

commit v3 on v1

--- a/solution.py
+++ b/solution.py
@@ -7,7 +7,7 @@
 from jax.experimental.pallas import tpu as pltpu
 from jax.sharding import PartitionSpec as P
 
-DOWN_CHUNKS = 2
+DOWN_CHUNKS = 4
 UP_CHUNKS = 2
 MESH = pl.DeviceIdType.MESH
 
@@ -189,8 +189,9 @@
     for a in range(row_index_ref.shape[0]):
         target = jnp.where(adapters == a, row_index_ref[a], target)
         scale = jnp.where(adapters == a, scales_ref[a], scale)
-    target_ref[...] = jnp.broadcast_to(target, target_ref.shape)
-    scale_ref[...] = jnp.broadcast_to(scale, scale_ref.shape)
+    spread = (rank2, rows_here)
+    target_ref[...] = jnp.broadcast_to(target.astype(jnp.float32), spread).T.astype(jnp.int32)
+    scale_ref[...] = jnp.broadcast_to(scale, spread).T
 
     def shrink(origin, first=False):
         weight = down_all[origin]
@@ -351,13 +352,13 @@
             pltpu.SemaphoreType.DMA((steps * (UP_CHUNKS + 1),)),
         ],
         compiler_params=pltpu.CompilerParams(
-            collective_id=0, has_side_effects=True, vmem_limit_bytes=32 * 1024 * 1024
+            collective_id=0, has_side_effects=True, vmem_limit_bytes=60 * 1024 * 1024
         ),
         name="lora_weights",
     )(
         adapter_row_index,
         adapter_scales,
-        request_adapter,
+        request_adapter.reshape(1, rows_here),
         hidden,
         down_weight_rows,
         query_up_weight,

time: 51.5 us -> 46.7 us (0.907)
  local copies, waits for them, and re-layouts: 8.48 us -> 3.91 us
    unnamed x15 -> x4, local copies, waits for them, and re-layouts: 8.48 us -> 3.91 us
where the time goes in v3:
time: 46.7 us; the launch traced here: 46.6 us
  Pallas kernels  42 us (90%)
  local copies, waits for them, and re-layouts  3.91 us (8%)
  between operations  0.65 us (1%)
    pallas_call x1, Pallas kernels, per_device_weights(): pl.pallas_call(functools.partial(lora_kernel, holders), out_shape=(jax.Sh...  42 us
    unnamed x4, local copies, waits for them, and re-layouts  3.91 us

profile of v3, /device:TPU:0, one launch (start us, length us, event | category | flops | bytes accessed | tf_op | source)
XLA Modules:
  0.0 46.6 jit_solution(2749758284293624759)
XLA Ops:
  0.6 42.0 %lora_weights.1 = (bf16[2,256,2048]{2,1,0:T(8,128)(2,1)}, bf16[2,256,256]{2,1,0:T(8,128)(2,1)}) custom-call(s32[4]{0:T(128)} %row_index_ref.1, f32[4]{0:T(128)} %scales_ref.1, s32[1,256]{1,0:T(1,128)} %bitcast.1, bf16[2,256,2048]{2,1,0:T(8,128)(2,1)} %hidden_hbm.1, bf16[1,128,2048]{2,1,0:T(8,128)(2,1)} %down_hbm.1, bf16[1,64,2048]{2,1,0:T(8,128)(2,1)} %query_hbm.1, ...), custom_call_target="tpu_custom_call" | custom-call | tf_op jit(solution)/shard_map/lora_weights/pallas_call | solution.py:323
  42.7 0.0 copy-start
  42.7 3.2 %copy.11 = bf16[2,256,2048]{2,1,0:T(8,128)(2,1)} copy(bf16[2,256,2048]{2,1,0:T(8,128)(2,1)} %get-tuple-element.4) | data formatting | bytes 4194304
  45.9 0.0 copy-done
  45.9 0.7 %copy.12 = bf16[2,256,256]{2,1,0:T(8,128)(2,1)} copy(bf16[2,256,256]{2,1,0:T(8,128)(2,1)S(1)} %copy-done) | data formatting | bytes 524288
Async XLA Ops:
  42.7 3.2 %copy-start = (bf16[2,256,256]{2,1,0:T(8,128)(2,1)S(1)}, bf16[2,256,256]{2,1,0:T(8,128)(2,1)}, u32[]{:S(2)}) copy-start(bf16[2,256,256]{2,1,0:T(8,128)(2,1)} %get-tuple-element.5) | copy-start | bytes 786436
